TPU v7x, 32 devices: a whole 2x2x4 slice. The times are simulated.
32 devices in a mesh: member: 2 (over y), tile: 4 (over z), nest: 2 (over x), lev: 2 (over core).
Axes of the slice: x: 2, y: 2, z: 4, core: 2. Of those that a mesh axis runs over, the one named last changes fastest.
Arguments:
- parent_field: float32 [10, 2, 256, 512], P('member', None, 'tile', ('nest', 'lev')), parts along dimension 0, may hold values from -6 to 6
- nest_fields: float32 [12, 5, 2, 384, 384], P(('member', 'nest'), None, None, 'tile', 'lev'), parts along dimension 0, may hold values from -6 to 6
- lateral_rate: float32 [5], replicated, may hold values from 0.02 to 0.12
- vertical_rate: float32 [5], replicated, may hold values from 0.02 to 0.12
- centres: int32 [6, 6, 2], P('member'), parts along dimension 0, may hold values from 64 to 448, as said below
- slot_storm: int32 [12], P('member'), parts along dimension 0, may hold values from 0 to 5, each once
Outputs:
- parent_final: float32 [10, 2, 256, 512], P('member', None, 'tile', ('nest', 'lev')), parts along dimension 0
- nest_final: float32 [12, 5, 2, 384, 384], P(('member', 'nest'), None, None, 'tile', 'lev'), parts along dimension 0
There are 2 independent parts, one for each index of `member`. A program takes and returns all parts, laid end to end along the dimension named above; an argument that names none is the same for every part. Nothing has to cross between parts.
Inputs may be any that keep to these rules, and one draw needn't show every extreme that they name: `centres`: from one step to the next the row of a centre changes by 1 to 2 cells in either direction and the column by at most 2 cells; rows stay within 64 to 192 and columns within 64 to 448. `slot_storm`: every storm occupies exactly one nest position.
All inputs are finite; a program needn't handle non-finite values.
Results may differ from a plain program's by a relative error of at most 0.0003.
Values sent between devices are 32-bit elements; how exact they have to be, the bound alone decides.
No kernel may reach another device: no remote copies, remote signals or barrier semaphores. Data moves between devices by JAX's collectives and lax.ppermute only.
A program may use at most 128 MiB of HBM per device.

v0:
```python
import jax
import jax.numpy as jnp
from jax import lax
from jax.sharding import PartitionSpec as P

FP = 128
BWP = 2
MOVE = 2


def extended(cells, sides, width):
    for axis, dim in sides:
        count = lax.axis_size(axis)
        ends = count - 1
        head = lax.slice_in_dim(cells, 0, width, axis=dim)
        tail = lax.slice_in_dim(cells, cells.shape[dim] - width, cells.shape[dim], axis=dim)
        cells = jnp.concatenate(
            [
                lax.ppermute(tail, axis, [(i, (i + 1) % count) for i in range(ends)]),
                cells,
                lax.ppermute(head, axis, [((i + 1) % count, i) for i in range(ends)]),
            ],
            axis=dim,
        )
    return cells


def tendency(padded, lateral_rate, vertical_rate):
    centre = padded[..., 1:-1, 1:-1, 1:-1]
    lateral = (
        padded[..., 1:-1, 2:, 1:-1]
        + padded[..., 1:-1, :-2, 1:-1]
        + padded[..., 1:-1, 1:-1, 2:]
        + padded[..., 1:-1, 1:-1, :-2]
        - 4.0 * centre
    )
    upright = padded[..., 2:, 1:-1, 1:-1] + padded[..., :-2, 1:-1, 1:-1] - 2.0 * centre
    change = (
        lateral_rate[:, None, None, None] * lateral + vertical_rate[:, None, None, None] * upright
    )
    return (centre, change)


def select_rows(picker, table):
    return jnp.sum(picker[:, :, None] * table[None, :, :], axis=1)


def column_block():
    return lax.axis_index("nest") * lax.axis_size("lev") + lax.axis_index("lev")


def extract(parent_now, anchors):
    fields, level_count, parent_rows, parent_cols = parent_now.shape
    padded = jnp.pad(parent_now, ((0, 0), (0, 0), (FP, FP), (FP, FP)))
    rel_rows = anchors[:, 0] - lax.axis_index("tile") * parent_rows + FP
    rel_cols = anchors[:, 1] - column_block() * parent_cols + FP
    zero_index = jnp.zeros((), jnp.int32)

    def single(corner):
        row_at = corner[0]
        col_at = corner[1]
        within = (
            (row_at >= 0)
            & (row_at <= FP + parent_rows)
            & (col_at >= 0)
            & (col_at <= FP + parent_cols)
        )
        row_at = jnp.clip(row_at, 0, FP + parent_rows)
        col_at = jnp.clip(col_at, 0, FP + parent_cols)
        south = lax.dynamic_slice(
            padded, (zero_index, zero_index, row_at, col_at), (fields, level_count, BWP, FP)
        )
        north = lax.dynamic_slice(
            padded,
            (zero_index, zero_index, row_at + FP - BWP, col_at),
            (fields, level_count, BWP, FP),
        )
        west = lax.dynamic_slice(
            padded, (zero_index, zero_index, row_at, col_at), (fields, level_count, FP, BWP)
        )
        east = lax.dynamic_slice(
            padded,
            (zero_index, zero_index, row_at, col_at + FP - BWP),
            (fields, level_count, FP, BWP),
        )
        sides = jnp.stack(
            [south, north, jnp.swapaxes(west, 2, 3), jnp.swapaxes(east, 2, 3)], axis=2
        )
        return jnp.where(within, sides.reshape(fields, level_count, 4 * BWP * FP), 0.0)

    corners = jnp.stack([rel_rows, rel_cols], axis=1)
    return lax.map(single, corners)


def per_device(parent_field, nest_fields, lateral_rate, vertical_rate, centres, slot_storm):
    fields, level_count, parent_rows, parent_cols = parent_field.shape
    slot_count = nest_fields.shape[0]
    strip_rows = nest_fields.shape[3]
    strip_cols = nest_fields.shape[4]
    storm_count = slot_storm.shape[0]
    steps_total = centres.shape[0] - 1
    tile_at = lax.axis_index("tile")
    nest_at = lax.axis_index("nest")
    lev_at = lax.axis_index("lev")
    nest_span = 3 * FP
    reach_rows = 3 * MOVE
    border = 3 * BWP
    zero_index = jnp.zeros((), jnp.int32)
    storm_ids = jnp.arange(storm_count, dtype=jnp.int32)
    pick_all = (slot_storm[:, None] == storm_ids[None, :]).astype(jnp.int32)
    owned = lax.dynamic_slice_in_dim(slot_storm, nest_at * slot_count, slot_count)
    pick_own = (owned[:, None] == storm_ids[None, :]).astype(jnp.int32)
    global_rows = tile_at * strip_rows + jnp.arange(strip_rows, dtype=jnp.int32)
    global_cols = lev_at * strip_cols + jnp.arange(strip_cols, dtype=jnp.int32)
    row_gap = jnp.minimum(global_rows, nest_span - 1 - global_rows)
    col_gap = jnp.minimum(global_cols, nest_span - 1 - global_cols)
    distance = jnp.minimum(row_gap[:, None], col_gap[None, :])
    weight = jnp.maximum(border - distance, 0).astype(jnp.float32) / jnp.float32(border)
    inside = (distance >= 1).astype(jnp.float32)
    coarse_rows = global_rows // 3
    coarse_cols = global_cols // 3
    south_index = jnp.clip(coarse_rows, 0, BWP - 1)
    north_index = jnp.clip(coarse_rows - (FP - BWP), 0, BWP - 1)
    west_index = jnp.clip(coarse_cols, 0, BWP - 1)
    east_index = jnp.clip(coarse_cols - (FP - BWP), 0, BWP - 1)
    near_south = (coarse_rows < BWP)[:, None]
    near_north = (coarse_rows >= FP - BWP)[:, None]
    near_west = (coarse_cols < BWP)[None, :]
    near_east = (coarse_cols >= FP - BWP)[None, :]

    def relocate(single, offset):
        return lax.dynamic_slice(
            single,
            (zero_index, zero_index, reach_rows + offset[0], reach_rows + offset[1]),
            (fields, level_count, strip_rows, strip_cols),
        )

    def across(zone, zone_index):
        picked = jnp.take(zone, zone_index, axis=3)
        return jnp.take(picked, coarse_cols, axis=4)

    def along(zone, zone_index):
        picked = jnp.take(zone, zone_index, axis=3)
        picked = jnp.take(picked, coarse_rows, axis=4)
        return jnp.swapaxes(picked, 3, 4)

    parent_now = parent_field
    nests_now = nest_fields
    for step_index in range(steps_total):
        padded = extended(parent_now, (("tile", 2), (("nest", "lev"), 3)), 1)
        padded = jnp.pad(padded, ((0, 0), (1, 1), (0, 0), (0, 0)))
        centre, change = tendency(padded, lateral_rate, vertical_rate)
        parent_now = centre + change
        later_pos = select_rows(pick_all, centres[step_index + 1])
        anchors = later_pos - FP // 2
        terms = extract(parent_now, anchors)
        totals = lax.psum(terms, ("tile", "nest", "lev"))
        boundary = lax.dynamic_slice_in_dim(totals, nest_at * slot_count, slot_count, 0)
        boundary = boundary.reshape(slot_count, fields, level_count, 4, BWP, FP)
        south_full = across(boundary[:, :, :, 0], south_index)
        north_full = across(boundary[:, :, :, 1], north_index)
        west_full = along(boundary[:, :, :, 2], west_index)
        east_full = along(boundary[:, :, :, 3], east_index)
        sides_full = jnp.where(near_west, west_full, jnp.where(near_east, east_full, 0.0))
        driving = jnp.where(near_south, south_full, jnp.where(near_north, north_full, sides_full))
        own_later = select_rows(pick_own, centres[step_index + 1])
        own_before = select_rows(pick_own, centres[step_index])
        offsets = 3 * (own_later - own_before)
        widened_nests = extended(nests_now, (("tile", 3), ("lev", 4)), reach_rows)
        shifted = jax.vmap(relocate)(widened_nests, offsets)
        source_rows = global_rows[None, :] + offsets[:, 0:1]
        source_cols = global_cols[None, :] + offsets[:, 1:2]
        rows_fine = (source_rows >= 0) & (source_rows < nest_span)
        cols_fine = (source_cols >= 0) & (source_cols < nest_span)
        keep_mask = (rows_fine[:, :, None] & cols_fine[:, None, :])[:, None, None, :, :]
        retained = jnp.where(keep_mask, shifted, driving)
        relaxed = retained + weight * (driving - retained)
        bordered = extended(relaxed, (("tile", 3), ("lev", 4)), 1)
        bordered = jnp.pad(bordered, ((0, 0), (0, 0), (1, 1), (0, 0), (0, 0)))
        centre, change = tendency(bordered, lateral_rate, vertical_rate)
        nests_now = relaxed + inside * change
    return (parent_now, nests_now)


def solution(mesh):
    placed = (
        P("member", None, "tile", ("nest", "lev")),
        P(("member", "nest"), None, None, "tile", "lev"),
        P(),
        P(),
        P("member", None, None),
        P("member"),
    )
    return jax.shard_map(
        per_device,
        mesh=mesh,
        in_specs=placed,
        out_specs=(
            P("member", None, "tile", ("nest", "lev")),
            P(("member", "nest"), None, None, "tile", "lev"),
        ),
        check_vma=False,
    )
```

profile of v0, /device:TPU:0, one launch (start us, length us, event | category | flops | bytes accessed | tf_op | source)
XLA Modules:
  0.0 790.2 jit_solution(10287252542518076452)
XLA Ops:
  9.4 5.6 collective-permute-start.1
  18.3 5.2 collective-permute-start.8
  47.2 5.5 copy.328
  58.2 6.7 collective-permute-start.7
  65.0 49.2 %while.32 = (s32[]{:T(128)}, f32[6,5,2,1024]{3,2,1,0:T(2,128)S(1)}, s32[6,2]{0,1:T(2,128)S(1)}, f32[5,2,320,384]{2,3,1,0:T(8,128)}, s32[]{:T(128)}, /*index=5*/s...) while((s32[]{:T(128)}, f32[6,5,2,1024]{3,2,1,0:T(2,128)S(1)}, ...), condition=%wide.region_5.6_spmd, body=%wide.region_4.5_spmd.sunk | while | flops 40981 | bytes 450935 | solution.py:92
  130.7 5.8 collective-permute-start.10
  136.6 49.5 %while.33 = (s32[]{:T(128)}, f32[6,5,2,1024]{3,2,1,0:T(2,128)S(1)}, s32[6,2]{0,1:T(2,128)S(1)}, f32[5,2,320,384]{2,3,1,0:T(8,128)}, s32[]{:T(128)}, /*index=5*/s...) while((s32[]{:T(128)}, f32[6,5,2,1024]{3,2,1,0:T(2,128)S(1)}, ...), condition=%wide.region_9.14_spmd, body=%wide.region_8.13_spmd.sunk | while | flops 40981 | bytes 450935 | solution.py:92
  186.9 8.2 %pad_maximum_fusion = f32[3,5,2,108,204]{3,2,4,1,0:T(2,128)S(1)} fusion(f32[3,5,2,108,6]{3,2,4,1,0:T(2,128)S(1)} %collective-permute-done.11, f32[3,5,2,6,192]{3,2,4,1,0:T(2,128)} %copy.329, f32[3,5,2,96,192]{3,2,4,1,0:T(2,128)} %copy.328, f32[3,5,2,6,192]{3,2,4,1,0:T(2,128)} %copy.327, f32[3,5,2,108,6]{3,2,4,1,0:T(2,128)} %collective-permute-done.10), kind=kLoop, calls=%fused_computation.46 | loop fusion | flops 2643840 | bytes 5287680 | tf_op jit(solution)/shard_map/concatenate | solution.py:17
  197.5 13.3 %while.34 = (s32[]{:T(128)}, f32[3,5,2,108,204]{3,2,4,1,0:T(2,128)S(1)}, s32[3,5]{1,0:T(4,128)S(1)}, f32[3,5,2,96,192]{3,2,1,0,4:T(2,128)}, s32[]{:T(128)}) while((s32[]{:T(128)}, f32[3,5,2,108,204]{3,2,4,1,0:T(2,128)S(1)}, s32[3,5]{1,0:T(4,128)S(1)}, f32[3,5,2,96,192]{3,2,1,0,4:T(2,128)}, s32[]{:T(128)}) %tuple.212), condition=%wide.while_cond, body=%wide.while_body.sunk | while | flops 2 | bytes 1967757 | solution.py:132
  210.8 70.3 %all-reduce.9.cloned.1.call-done = (f32[6,5,2,1024]{3,2,1,0:T(2,128)}, f32[6,5,2,1024]{3,2,1,0:T(2,128)}) async-done(((f32[6,5,2,1024]{3,2,1,0:T(2,128)}, f32[6,5,2,1024]{3,2,1,0:T(2,128)}), (f32[6,5,2,1024]{3,2,1,0:T(2,128)}, f32[6,5,2,1024]{3,2,1,0:T(2,128)})) %all-reduce.9.cloned.1.call-update) | async-done | bytes 491536 | tf_op jit(solution)/shard_map/psum | solution.py:157
  282.5 12.2 %gather_fusion.14 = f32[192,3,5,2,128]{4,3,2,1,0:T(2,128)S(1)} fusion(f32[3,5,2,2,128]{4,2,3,1,0:T(2,128)S(1)} %bitcast.166, s32[1024]{0:T(1024)S(1)} %pad_clamp_fusion), kind=kCustom, calls=%fused_computation.12.clone | custom fusion | bytes 5899008 | tf_op jit(solution)/shard_map/jit(_take)/gather | solution.py:143
  294.8 11.2 %gather_fusion.6 = f32[192,3,5,2,128]{4,3,2,1,0:T(2,128)} fusion(f32[3,5,2,2,128]{4,2,3,1,0:T(2,128)S(1)} %bitcast.167, s32[1024]{0:T(1024)S(1)} %pad_clamp_fusion), kind=kCustom, calls=%fused_computation.10.clone | custom fusion | bytes 5899008 | tf_op jit(solution)/shard_map/jit(_take)/gather | solution.py:143
  306.0 6.8 select_bitcast_fusion
  312.8 7.9 %copy.342 = f32[3,5,2,192,128]{3,2,4,1,0:T(2,128)} copy(f32[3,5,2,192,128]{4,2,1,0,3:T(2,128)} %get-tuple-element.471) | data formatting | bytes 5898240 | tf_op jit(solution)/shard_map/jit(_take)/select_n | solution.py:143
  320.7 11.0 %gather_fusion.7 = f32[96,3,5,2,192]{4,3,2,1,0:T(2,128)S(1)} fusion(f32[3,5,2,192,128]{3,2,4,1,0:T(2,128)} %copy.342, s32[1024]{0:T(1024)S(1)} %pad_clamp_fusion.1), kind=kCustom, calls=%fused_computation.13.clone | custom fusion | bytes 4424064 | tf_op jit(solution)/shard_map/jit(_take)/gather | solution.py:144
  331.7 5.2 copy.343
  337.0 12.2 %gather_fusion.12 = f32[192,3,5,2,128]{4,3,2,1,0:T(2,128)S(1)} fusion(f32[3,5,2,2,128]{4,2,3,1,0:T(2,128)S(1)} %bitcast.169, s32[1024]{0:T(1024)S(1)} %pad_clamp_fusion.2), kind=kCustom, calls=%fused_computation.11.clone | custom fusion | bytes 5899008 | tf_op jit(solution)/shard_map/jit(_take)/gather | solution.py:143
  349.2 10.6 %gather_fusion.4 = f32[192,3,5,2,128]{4,3,2,1,0:T(2,128)} fusion(f32[3,5,2,2,128]{4,2,3,1,0:T(2,128)S(1)} %bitcast.168, s32[1024]{0:T(1024)S(1)} %pad_clamp_fusion.2), kind=kCustom, calls=%fused_computation.2.clone | custom fusion | bytes 5899008 | tf_op jit(solution)/shard_map/jit(_take)/gather | solution.py:143
  359.9 6.8 select_bitcast_fusion.1
  366.7 8.0 %copy.339 = f32[3,5,2,192,128]{3,2,4,1,0:T(2,128)} copy(f32[3,5,2,192,128]{4,2,1,0,3:T(2,128)} %get-tuple-element.469) | data formatting | bytes 5898240 | tf_op jit(solution)/shard_map/jit(_take)/select_n | solution.py:143
  374.6 11.1 %gather_fusion.5 = f32[96,3,5,2,192]{4,3,2,1,0:T(2,128)S(1)} fusion(f32[3,5,2,192,128]{3,2,4,1,0:T(2,128)} %copy.339, s32[1024]{0:T(1024)S(1)} %pad_clamp_fusion.1), kind=kCustom, calls=%fused_computation.3.clone | custom fusion | bytes 4424064 | tf_op jit(solution)/shard_map/jit(_take)/gather | solution.py:144
  385.8 5.2 copy.340
  409.8 4.8 select_bitcast_fusion.5
  419.1 12.1 %gather_fusion.3 = f32[192,3,5,2,96]{4,3,2,1,0:T(2,128)} fusion(f32[3,5,2,96,128]{3,2,4,1,0:T(2,128)S(1)} %copy.337, s32[1024]{0:T(1024)S(1)} %pad_clamp_fusion.4), kind=kCustom, calls=%fused_computation.7.clone | custom fusion | bytes 4424448 | tf_op jit(solution)/shard_map/jit(_take)/gather | solution.py:140
  431.3 14.2 %gather_fusion.1 = f32[192,3,5,2,96]{4,3,2,1,0:T(2,128)} fusion(f32[3,5,2,96,128]{3,2,4,1,0:T(2,128)} %copy.335, s32[1024]{0:T(1024)S(1)} %pad_clamp_fusion.4), kind=kCustom, calls=%fused_computation.1.clone | custom fusion | bytes 4424448 | tf_op jit(solution)/shard_map/jit(_take)/gather | solution.py:140
  445.5 9.3 %multiply_add_fusion.3 = f32[3,5,2,96,192]{3,2,1,0,4:T(2,128)S(1)} fusion(f32[3,5,2,96,192]{3,2,1,0,4:T(2,128)} %get-tuple-element.219, pred[3,96,192]{1,0,2:T(4,128)(4,1)S(1)} %copy-done.13, f32[96,3,5,2,192]{0,3,2,1,4:T(2,128)} %copy.343, pred[192]{0:T(512)(128)(4,1)S(1)} %copy-done.18, f32[96,3,5,2,192]{0,3,2,1,4:T(2,128)} %copy.340, ...), kind=kLoop, calls=%fused_computation.97 | loop fusion | flops 6635520 | bytes 13400928 | tf_op jit(solution)/shard_map/add | solution.py:177
  454.8 6.7 fusion.56
  488.4 8.4 %select_maximum_fusion.4 = f32[3,5,4,98,194]{3,2,1,0,4:T(4,128)S(1)} fusion(f32[3,5,2,98,1]{3,2,1,0,4:T(2,128)S(1)} %collective-permute-done.14, f32[3,5,2,98,1]{3,2,1,0,4:T(2,128)S(1)} %collective-permute-done.15, f32[3,5,2,1,192]{3,2,1,0,4:T(2,128)S(1)} %copy-done.2, f32[3,5,2,96,192]{3,2,1,0,4:T(2,128)S(1)} %multiply_add_fusion.3, ...), kind=kLoop, calls=%fused_computation.41 | loop fusion | flops 13688640 | bytes 6844320 | tf_op jit(solution)/shard_map/concatenate | solution.py:17
  496.8 37.4 %multiply_add_fusion.2 = f32[3,5,2,96,192]{3,2,1,0,4:T(2,128)S(1)} fusion(f32[3,5,2,96,192]{3,2,1,0,4:T(2,128)S(1)} %multiply_add_fusion.3, f32[3,5,4,98,194]{3,2,1,0,4:T(4,128)S(1)} %select_maximum_fusion.4, f32[3,5,2,1,192]{3,2,1,0,4:T(2,128)S(1)} %copy-done.2, f32[3,5,2,1,192]{3,2,1,0,4:T(2,128)S(1)} %copy-done.4, ...), kind=kLoop, calls=%fused_computation.96 | loop fusion | flops 11612160 | bytes 8990728 | tf_op jit(solution)/shard_map/add | solution.py:181
  534.2 5.6 fusion.55
  548.4 5.2 collective-permute-start.16
  569.3 8.2 %copy.367 = f32[3,5,2,192,128]{3,2,4,1,0:T(2,128)} copy(f32[3,5,2,192,128]{4,2,1,0,3:T(2,128)} %get-tuple-element.470) | data formatting | bytes 5898240 | tf_op jit(solution)/shard_map/jit(_take)/select_n | solution.py:143
  577.5 10.8 %gather_fusion.15 = f32[96,3,5,2,192]{4,3,2,1,0:T(2,128)} fusion(f32[3,5,2,192,128]{3,2,4,1,0:T(2,128)} %copy.367, s32[1024]{0:T(1024)S(1)} %pad_clamp_fusion.1), kind=kCustom, calls=%fused_computation.15.clone | custom fusion | bytes 4424064 | tf_op jit(solution)/shard_map/jit(_take)/gather | solution.py:144
  588.3 7.3 copy.368
  595.6 8.0 %copy.364 = f32[3,5,2,192,128]{3,2,4,1,0:T(2,128)} copy(f32[3,5,2,192,128]{4,2,1,0,3:T(2,128)} %get-tuple-element.468) | data formatting | bytes 5898240 | tf_op jit(solution)/shard_map/jit(_take)/select_n | solution.py:143
  603.6 10.8 %gather_fusion.13 = f32[96,3,5,2,192]{4,3,2,1,0:T(2,128)} fusion(f32[3,5,2,192,128]{3,2,4,1,0:T(2,128)} %copy.364, s32[1024]{0:T(1024)S(1)} %pad_clamp_fusion.1), kind=kCustom, calls=%fused_computation.14.clone | custom fusion | bytes 4424064 | tf_op jit(solution)/shard_map/jit(_take)/gather | solution.py:144
  614.3 7.3 copy.365
  626.1 14.1 %gather_fusion.11 = f32[192,3,5,2,96]{4,3,2,1,0:T(2,128)} fusion(f32[3,5,2,96,128]{3,2,4,1,0:T(2,128)} %copy.362, s32[1024]{0:T(1024)S(1)} %pad_clamp_fusion.4), kind=kCustom, calls=%fused_computation.9.clone | custom fusion | bytes 4424448 | tf_op jit(solution)/shard_map/jit(_take)/gather | solution.py:140
  644.7 13.6 %gather_fusion.9 = f32[192,3,5,2,96]{4,3,2,1,0:T(2,128)} fusion(f32[3,5,2,96,128]{3,2,4,1,0:T(2,128)} %copy.360, s32[1024]{0:T(1024)S(1)} %pad_clamp_fusion.4), kind=kCustom, calls=%fused_computation.8.clone | custom fusion | bytes 4424448 | tf_op jit(solution)/shard_map/jit(_take)/gather | solution.py:140
  658.4 9.2 %pad_maximum_fusion.1 = f32[3,5,2,108,204]{3,2,1,0,4:T(2,128)} fusion(f32[3,5,2,108,6]{3,2,1,0,4:T(2,128)S(1)} %collective-permute-done.19, f32[3,5,2,6,192]{3,2,1,0,4:T(2,128)} %copy.354, f32[3,5,2,96,192]{3,2,1,0,4:T(2,128)S(1)} %copy-done.1, f32[3,5,2,6,192]{3,2,1,0,4:T(2,128)} %copy.353, f32[3,5,2,108,6]{3,2,1,0,4:T(2,128)} %collective-permute-done.18), kind=kLoop, calls=%fused_computation.47 | loop fusion | flops 2643840 | bytes 5287680 | tf_op jit(solution)/shard_map/concatenate | solution.py:17
  668.5 18.0 %while.35 = (s32[]{:T(128)}, f32[3,5,2,108,204]{3,2,1,0,4:T(2,128)}, s32[3,5]{1,0:T(4,128)}, f32[3,5,2,96,192]{3,2,1,0,4:T(2,128)S(1)}, s32[]{:T(128)}) while((s32[]{:T(128)}, f32[3,5,2,108,204]{3,2,1,0,4:T(2,128)}, s32[3,5]{1,0:T(4,128)}, f32[3,5,2,96,192]{3,2,1,0,4:T(2,128)S(1)}, s32[]{:T(128)}) %tuple.221), condition=%wide.while_cond.1, body=%wide.while_body.1.sunk | while | flops 2 | bytes 1720473 | solution.py:132
  681.8 4.7 dynamic-slice_dynamic-update-slice_fusion.2
  688.1 9.3 %multiply_add_fusion.1 = f32[3,5,2,96,192]{3,2,1,0,4:T(2,128)S(1)} fusion(f32[3,5,2,96,192]{3,2,1,0,4:T(2,128)} %copy-done.7, pred[3,96,192]{1,0,2:T(4,128)(4,1)S(1)} %broadcast_and_fusion.1, f32[96,3,5,2,192]{0,3,2,1,4:T(2,128)} %copy.368, pred[192]{0:T(512)(128)(4,1)S(1)} %copy-done.19, f32[96,3,5,2,192]{0,3,2,1,4:T(2,128)} %copy.365, ...), kind=kLoop, calls=%fused_computation.95 | loop fusion | flops 6635520 | bytes 13400928 | tf_op jit(solution)/shard_map/add | solution.py:177
  697.4 6.6 fusion.54
  713.2 4.7 collective-permute-start.21
  731.0 8.4 %select_maximum_fusion = f32[3,5,4,98,194]{3,2,1,0,4:T(4,128)S(1)} fusion(f32[3,5,2,98,1]{3,2,1,0,4:T(2,128)S(1)} %collective-permute-done.22, f32[3,5,2,98,1]{3,2,1,0,4:T(2,128)S(1)} %collective-permute-done.23, f32[3,5,2,1,192]{3,2,1,0,4:T(2,128)S(1)} %copy-done.3, f32[3,5,2,96,192]{3,2,1,0,4:T(2,128)S(1)} %multiply_add_fusion.1, ...), kind=kLoop, calls=%fused_computation.37 | loop fusion | flops 13688640 | bytes 6844320 | tf_op jit(solution)/shard_map/concatenate | solution.py:17
  739.4 38.3 %multiply_add_fusion = f32[3,5,2,96,192]{3,2,1,0,4:T(2,128)} fusion(f32[3,5,2,96,192]{3,2,1,0,4:T(2,128)S(1)} %multiply_add_fusion.1, f32[3,5,4,98,194]{3,2,1,0,4:T(4,128)S(1)} %select_maximum_fusion, f32[3,5,2,1,192]{3,2,1,0,4:T(2,128)S(1)} %copy-done.3, f32[3,5,2,1,192]{3,2,1,0,4:T(2,128)S(1)} %copy-done.5, ...), kind=kLoop, calls=%fused_computation.94 | loop fusion | flops 11612160 | bytes 8990728 | tf_op jit(solution)/shard_map/add | solution.py:181
  777.6 5.5 copy.376
  (360 shorter events, 242.4 us)
Async XLA Ops:
  7.2 33.1 %copy-start.8 = (f32[5,2,64,128]{3,2,1,0:T(8,128)S(1)}, f32[5,2,64,128]{3,2,1,0:T(8,128)}, u32[]{:S(2)}) copy-start(f32[5,2,64,128]{3,2,1,0:T(8,128)} %param.18) | copy-start | bytes 983044
  7.2 273.9 %all-reduce.9.cloned.1.call-start = ((), (), s32[]{:S(2)}) async-start(), calls=%async_computation | async-start | bytes 983040 | tf_op jit(solution)/shard_map/psum | solution.py:157
  8.1 25.3 %collective-permute-start = (f32[5,2,1,128]{3,2,1,0:T(1,128)S(1)}, f32[5,2,1,128]{3,2,1,0:T(1,128)S(1)}, u32[]{:S(2)}, u32[]{:S(2)}) collective-permute-start(f32[5,2,1,128]{3,2,1,0:T(1,128)S(1)} %get-tuple-element.438), channel_id=1, source_target_pairs={{4,0},{8,4},{12,8},{5,1},{9,5},{13,9},{6,2},{10,6},{14,10},{7,3},{... | collective-permute-start | bytes 15368 | tf_op jit(solution)/shard_map/ppermute | solution.py:21
  9.4 24.0 %collective-permute-start.1 = (f32[5,2,1,128]{3,2,1,0:T(1,128)S(1)}, f32[5,2,1,128]{3,2,1,0:T(1,128)S(1)}, u32[]{:S(2)}, u32[]{:S(2)}) collective-permute-start(f32[5,2,1,128]{3,2,1,0:T(1,128)S(1)} %get-tuple-element.437), channel_id=1, source_target_pairs={{0,4},{4,8},{8,12},{1,5},{5,9},{9,13},{2,6},{6,10},{10,14},{3,7},{... | collective-permute-start | bytes 15368 | tf_op jit(solution)/shard_map/ppermute | solution.py:19
  16.1 24.5 %copy-start.14 = (f32[5]{0:T(128)S(1)}, f32[5]{0:T(128)}, u32[]{:S(2)}) copy-start(f32[5]{0:T(128)} %param.21) | copy-start | bytes 64
  16.2 24.5 %copy-start.15 = (f32[5]{0:T(128)S(1)}, f32[5]{0:T(128)}, u32[]{:S(2)}) copy-start(f32[5]{0:T(128)} %param.20) | copy-start | bytes 64
  16.2 102.9 %collective-permute-start.9 = (f32[3,5,2,6,192]{4,2,3,1,0:T(2,128)S(1)}, f32[3,5,2,6,192]{4,2,3,1,0:T(2,128)}, u32[]{:S(2)}, u32[]{:S(2)}) collective-permute-start(f32[3,5,2,6,192]{4,2,3,1,0:T(2,128)S(1)} %copy.384), channel_id=1, source_target_pairs={{4,0},{8,4},{12,8},{5,1},{9,5},{13,9},{6,2},{10,6},{14,10},{7,3},{... | collective-permute-start | bytes 414728 | tf_op jit(solution)/shard_map/ppermute | solution.py:21
  18.3 105.0 %collective-permute-start.8 = (f32[3,5,2,6,192]{4,2,3,1,0:T(2,128)}, f32[3,5,2,6,192]{4,2,3,1,0:T(2,128)}, u32[]{:S(2)}, u32[]{:S(2)}) collective-permute-start(f32[3,5,2,6,192]{4,2,3,1,0:T(2,128)} %copy.383), channel_id=1, source_target_pairs={{0,4},{4,8},{8,12},{1,5},{5,9},{9,13},{2,6},{6,10},{10,14},{3,7},{... | collective-permute-start | bytes 414728 | tf_op jit(solution)/shard_map/ppermute | solution.py:19
  25.9 15.3 %copy-start.28 = (s32[96]{0:T(128)}, s32[96]{0:T(128)S(1)}, u32[]{:S(2)}) copy-start(s32[96]{0:T(128)S(1)} %get-tuple-element.495) | copy-start | bytes 1156
  34.6 4.4 collective-permute-start.2
  35.9 4.3 collective-permute-start.3
  39.0 406.5 %copy-start.24 = (pred[192]{0:T(512)(128)(4,1)}, pred[192]{0:T(512)(128)(4,1)S(1)}, u32[]{:S(2)}) copy-start(pred[192]{0:T(512)(128)(4,1)S(1)} %broadcast_compare_fusion.1) | copy-start | bytes 580
  41.3 14.7 %collective-permute-start.4 = (f32[5,2,1,128]{3,2,1,0:T(1,128)S(1)}, f32[5,2,1,128]{3,2,1,0:T(1,128)S(1)}, u32[]{:S(2)}, u32[]{:S(2)}) collective-permute-start(f32[5,2,1,128]{3,2,1,0:T(1,128)S(1)} %get-tuple-element.436), channel_id=1, source_target_pairs={{4,0},{8,4},{12,8},{5,1},{9,5},{13,9},{6,2},{10,6},{14,10},{7,3},{... | collective-permute-start | bytes 15368 | tf_op jit(solution)/shard_map/ppermute | solution.py:21
  42.6 13.4 %collective-permute-start.5 = (f32[5,2,1,128]{3,2,1,0:T(1,128)S(1)}, f32[5,2,1,128]{3,2,1,0:T(1,128)S(1)}, u32[]{:S(2)}, u32[]{:S(2)}) collective-permute-start(f32[5,2,1,128]{3,2,1,0:T(1,128)S(1)} %get-tuple-element.435), channel_id=1, source_target_pairs={{0,4},{4,8},{8,12},{1,5},{5,9},{9,13},{2,6},{6,10},{10,14},{3,7},{... | collective-permute-start | bytes 15368 | tf_op jit(solution)/shard_map/ppermute | solution.py:19
  47.2 398.3 %copy-start.26 = (pred[96]{0:T(512)(128)(4,1)}, pred[96]{0:T(512)(128)(4,1)S(1)}, u32[]{:S(2)}) copy-start(pred[96]{0:T(512)(128)(4,1)S(1)} %broadcast_compare_fusion.3) | copy-start | bytes 292
  56.9 57.3 %collective-permute-start.6 = (f32[5,2,66,1]{3,2,1,0:T(8,128)}, f32[5,2,66,1]{3,2,1,0:T(8,128)S(1)}, u32[]{:S(2)}, u32[]{:S(2)}) collective-permute-start(f32[5,2,66,1]{3,2,1,0:T(8,128)} %get-tuple-element.432), channel_id=1, source_target_pairs={{1,0},{2,1},{3,2},{5,4},{6,5},{7,6},{9,8},{10,9},{11,10},{13,12},{... | collective-permute-start | bytes 7928 | tf_op jit(solution)/shard_map/ppermute | solution.py:21
  58.2 56.0 %collective-permute-start.7 = (f32[5,2,66,1]{3,2,1,0:T(8,128)S(1)}, f32[5,2,66,1]{3,2,1,0:T(8,128)S(1)}, u32[]{:S(2)}, u32[]{:S(2)}) collective-permute-start(f32[5,2,66,1]{3,2,1,0:T(8,128)S(1)} %get-tuple-element.431), channel_id=1, source_target_pairs={{0,1},{1,2},{2,3},{4,5},{5,6},{6,7},{8,9},{9,10},{10,11},{12,13},{... | collective-permute-start | bytes 7928 | tf_op jit(solution)/shard_map/ppermute | solution.py:19
  119.1 8.2 %copy-start.6 = (f32[3,5,2,96,192]{3,2,4,1,0:T(2,128)S(1)}, f32[3,5,2,96,192]{3,2,4,1,0:T(2,128)}, u32[]{:S(2)}) copy-start(f32[3,5,2,96,192]{3,2,4,1,0:T(2,128)} %copy.328) | copy-start | bytes 6635524
  129.4 57.4 %collective-permute-start.11 = (f32[3,5,2,108,6]{3,2,4,1,0:T(2,128)}, f32[3,5,2,108,6]{3,2,4,1,0:T(2,128)S(1)}, u32[]{:S(2)}, u32[]{:S(2)}) collective-permute-start(f32[3,5,2,108,6]{3,2,4,1,0:T(2,128)} %get-tuple-element.422), channel_id=1, source_target_pairs={{1,0},{3,2},{5,4},{7,6},{9,8},{11,10},{13,12},{15,14},{17,16},{19,... | collective-permute-start | bytes 233288 | tf_op jit(solution)/shard_map/ppermute | solution.py:21
  130.7 56.1 %collective-permute-start.10 = (f32[3,5,2,108,6]{3,2,4,1,0:T(2,128)S(1)}, f32[3,5,2,108,6]{3,2,4,1,0:T(2,128)}, u32[]{:S(2)}, u32[]{:S(2)}) collective-permute-start(f32[3,5,2,108,6]{3,2,4,1,0:T(2,128)S(1)} %get-tuple-element.421), channel_id=1, source_target_pairs={{0,1},{2,3},{4,5},{6,7},{8,9},{10,11},{12,13},{14,15},{16,17},{18,... | collective-permute-start | bytes 233288 | tf_op jit(solution)/shard_map/ppermute | solution.py:19
  294.8 11.3 %copy-start.34 = (pred[192]{0:T(512)(128)(4,1)S(1)}, pred[192]{0:T(512)(128)(4,1)}, u32[]{:S(2)}) copy-start(pred[192]{0:T(512)(128)(4,1)} %get-tuple-element.490) | copy-start | bytes 580
  349.2 10.6 %copy-start.33 = (pred[192]{0:T(512)(128)(4,1)S(1)}, pred[192]{0:T(512)(128)(4,1)}, u32[]{:S(2)}) copy-start(pred[192]{0:T(512)(128)(4,1)} %get-tuple-element.491) | copy-start | bytes 580
  431.3 14.2 %copy-start.12 = (f32[96,192]{0,1:T(8,128)S(1)}, f32[96,192]{0,1:T(8,128)}, u32[]{:S(2)}) copy-start(f32[96,192]{0,1:T(8,128)} %fusion.42) | copy-start | bytes 221188
  431.3 14.2 %copy-start.13 = (pred[3,96,192]{1,0,2:T(4,128)(4,1)S(1)}, pred[3,96,192]{1,0,2:T(4,128)(4,1)}, u32[]{:S(2)}) copy-start(pred[3,96,192]{1,0,2:T(4,128)(4,1)} %broadcast_and_fusion) | copy-start | bytes 165892
  431.3 14.2 %copy-start.16 = (pred[192]{0:T(512)(128)(4,1)S(1)}, pred[192]{0:T(512)(128)(4,1)}, u32[]{:S(2)}) copy-start(pred[192]{0:T(512)(128)(4,1)} %get-tuple-element.492) | copy-start | bytes 580
  431.3 14.2 %copy-start.18 = (pred[192]{0:T(512)(128)(4,1)S(1)}, pred[192]{0:T(512)(128)(4,1)}, u32[]{:S(2)}) copy-start(pred[192]{0:T(512)(128)(4,1)} %get-tuple-element.493) | copy-start | bytes 580
  431.3 14.2 %copy-start.20 = (pred[96]{0:T(512)(128)(4,1)S(1)}, pred[96]{0:T(512)(128)(4,1)}, u32[]{:S(2)}) copy-start(pred[96]{0:T(512)(128)(4,1)} %get-tuple-element.476) | copy-start | bytes 292
  431.3 14.2 %copy-start.22 = (pred[96]{0:T(512)(128)(4,1)S(1)}, pred[96]{0:T(512)(128)(4,1)}, u32[]{:S(2)}) copy-start(pred[96]{0:T(512)(128)(4,1)} %get-tuple-element.479) | copy-start | bytes 292
  465.5 9.9 %collective-permute-start.12 = (f32[3,5,2,1,192]{4,2,3,1,0:T(2,128)S(1)}, f32[3,5,2,1,192]{4,2,3,1,0:T(2,128)S(1)}, u32[]{:S(2)}, u32[]{:S(2)}) collective-permute-start(f32[3,5,2,1,192]{4,2,3,1,0:T(2,128)S(1)} %copy.345), channel_id=1, source_target_pairs={{4,0},{8,4},{12,8},{5,1},{9,5},{13,9},{6,2},{10,6},{14,10},{7,3},{... | collective-permute-start | bytes 69128 | tf_op jit(solution)/shard_map/ppermute | solution.py:21
  470.8 7.8 collective-permute-start.13
  483.1 4.6 collective-permute-start.14
  484.6 3.9 collective-permute-start.15
  543.8 10.6 %collective-permute-start.17 = (f32[3,5,2,6,192]{4,2,3,1,0:T(2,128)S(1)}, f32[3,5,2,6,192]{4,2,3,1,0:T(2,128)S(1)}, u32[]{:S(2)}, u32[]{:S(2)}) collective-permute-start(f32[3,5,2,6,192]{4,2,3,1,0:T(2,128)S(1)} %copy.352), channel_id=1, source_target_pairs={{4,0},{8,4},{12,8},{5,1},{9,5},{13,9},{6,2},{10,6},{14,10},{7,3},{... | collective-permute-start | bytes 414728 | tf_op jit(solution)/shard_map/ppermute | solution.py:21
  548.4 9.3 %collective-permute-start.16 = (f32[3,5,2,6,192]{4,2,3,1,0:T(2,128)}, f32[3,5,2,6,192]{4,2,3,1,0:T(2,128)}, u32[]{:S(2)}, u32[]{:S(2)}) collective-permute-start(f32[3,5,2,6,192]{4,2,3,1,0:T(2,128)} %copy.351), channel_id=1, source_target_pairs={{0,4},{4,8},{8,12},{1,5},{5,9},{9,13},{2,6},{6,10},{10,14},{3,7},{... | collective-permute-start | bytes 414728 | tf_op jit(solution)/shard_map/ppermute | solution.py:19
  554.4 7.6 copy-start.1
  562.0 7.1 copy-start.30
  564.1 94.3 %collective-permute-start.19 = (f32[3,5,2,108,6]{3,2,1,0,4:T(2,128)}, f32[3,5,2,108,6]{3,2,1,0,4:T(2,128)S(1)}, u32[]{:S(2)}, u32[]{:S(2)}) collective-permute-start(f32[3,5,2,108,6]{3,2,1,0,4:T(2,128)} %get-tuple-element.418), channel_id=1, source_target_pairs={{1,0},{3,2},{5,4},{7,6},{9,8},{11,10},{13,12},{15,14},{17,16},{19,... | collective-permute-start | bytes 233288 | tf_op jit(solution)/shard_map/ppermute | solution.py:21
  565.4 93.0 %collective-permute-start.18 = (f32[3,5,2,108,6]{3,2,1,0,4:T(2,128)S(1)}, f32[3,5,2,108,6]{3,2,1,0,4:T(2,128)}, u32[]{:S(2)}, u32[]{:S(2)}) collective-permute-start(f32[3,5,2,108,6]{3,2,1,0,4:T(2,128)S(1)} %get-tuple-element.417), channel_id=1, source_target_pairs={{0,1},{2,3},{4,5},{6,7},{8,9},{10,11},{12,13},{14,15},{16,17},{18,... | collective-permute-start | bytes 233288 | tf_op jit(solution)/shard_map/ppermute | solution.py:19
  668.4 19.6 %copy-start.17 = (pred[192]{0:T(512)(128)(4,1)S(1)}, pred[192]{0:T(512)(128)(4,1)}, u32[]{:S(2)}) copy-start(pred[192]{0:T(512)(128)(4,1)} %get-tuple-element.492) | copy-start | bytes 580
  668.4 19.6 %copy-start.19 = (pred[192]{0:T(512)(128)(4,1)S(1)}, pred[192]{0:T(512)(128)(4,1)}, u32[]{:S(2)}) copy-start(pred[192]{0:T(512)(128)(4,1)} %get-tuple-element.493) | copy-start | bytes 580
  668.4 19.6 %copy-start.21 = (pred[96]{0:T(512)(128)(4,1)S(1)}, pred[96]{0:T(512)(128)(4,1)}, u32[]{:S(2)}) copy-start(pred[96]{0:T(512)(128)(4,1)} %get-tuple-element.476) | copy-start | bytes 292
  668.4 19.6 %copy-start.23 = (pred[96]{0:T(512)(128)(4,1)S(1)}, pred[96]{0:T(512)(128)(4,1)}, u32[]{:S(2)}) copy-start(pred[96]{0:T(512)(128)(4,1)} %get-tuple-element.479) | copy-start | bytes 292
  668.4 19.6 %copy-start.25 = (pred[192]{0:T(512)(128)(4,1)S(1)}, pred[192]{0:T(512)(128)(4,1)}, u32[]{:S(2)}) copy-start(pred[192]{0:T(512)(128)(4,1)} %copy-done.24) | copy-start | bytes 580
  668.5 19.6 %copy-start.27 = (pred[96]{0:T(512)(128)(4,1)S(1)}, pred[96]{0:T(512)(128)(4,1)}, u32[]{:S(2)}) copy-start(pred[96]{0:T(512)(128)(4,1)} %copy-done.26) | copy-start | bytes 292
  707.9 10.0 %collective-permute-start.20 = (f32[3,5,2,1,192]{4,2,3,1,0:T(2,128)S(1)}, f32[3,5,2,1,192]{4,2,3,1,0:T(2,128)S(1)}, u32[]{:S(2)}, u32[]{:S(2)}) collective-permute-start(f32[3,5,2,1,192]{4,2,3,1,0:T(2,128)S(1)} %copy.370), channel_id=1, source_target_pairs={{4,0},{8,4},{12,8},{5,1},{9,5},{13,9},{6,2},{10,6},{14,10},{7,3},{... | collective-permute-start | bytes 69128 | tf_op jit(solution)/shard_map/ppermute | solution.py:21
  713.2 8.0 %collective-permute-start.21 = (f32[3,5,2,1,192]{4,2,3,1,0:T(2,128)S(1)}, f32[3,5,2,1,192]{4,2,3,1,0:T(2,128)S(1)}, u32[]{:S(2)}, u32[]{:S(2)}) collective-permute-start(f32[3,5,2,1,192]{4,2,3,1,0:T(2,128)S(1)} %copy.372), channel_id=1, source_target_pairs={{0,4},{4,8},{8,12},{1,5},{5,9},{9,13},{2,6},{6,10},{10,14},{3,7},{... | collective-permute-start | bytes 69128 | tf_op jit(solution)/shard_map/ppermute | solution.py:19
  725.7 4.5 collective-permute-start.22
  727.1 3.9 collective-permute-start.23
  (12 other events, 56.0 us)
Sparse Core Ops, SparseCore 0:
  187.0 94.0 all-reduce.8
where the time goes:
time: 801 us; the launch traced here: 790 us
  local copies, waits for them, and re-layouts  416 us (52%)
  other arithmetic  168 us (21%)
  waiting for transfers between devices  73.1 us (9%)
  starting transfers between devices  70.8 us (9%)
  loops' own time  46.6 us (6%)
  between operations  15.3 us (2%)
    add x2, other arithmetic, per_device(): nests_now = relaxed + inside * change  75.6 us
    psum x1, waiting for transfers between devices, per_device(): totals = lax.psum(terms, ('tile', 'nest', 'lev'))  70.3 us
    gather x8, local copies, waits for them, and re-layouts, along(): picked = jnp.take(picked, coarse_rows, axis=4)  68.6 us
    ppermute x12, starting transfers between devices, extended(): lax.ppermute(tail, axis, [(i, (i + 1) % count) for i in range(ends)])  55 us
    gather x4, local copies, waits for them, and re-layouts, across(): return jnp.take(picked, coarse_cols, axis=4)  54 us
    another operation x2, loops' own time, extract(): return lax.map(single, corners)  46.6 us
    gather x4, local copies, waits for them, and re-layouts, along(): picked = jnp.take(zone, zone_index, axis=3)  46.3 us
    concatenate x10, other arithmetic, extended(): jnp.concatenate([lax.ppermute(tail, axis, [(i, (i + 1) % count) for i in...  38.2 us
  transfers between devices with their start and end apart: 25, of which 4 were waited for; matrix products, arithmetic and copies ran while one was open for 28% of the time, Pallas kernels for 0%

commit v1 on v0

--- a/solution.py
+++ b/solution.py
@@ -154,7 +154,7 @@
         later_pos = select_rows(pick_all, centres[step_index + 1])
         anchors = later_pos - FP // 2
         terms = extract(parent_now, anchors)
-        totals = lax.psum(terms, ("tile", "nest", "lev"))
+        totals = jnp.sum(lax.all_gather(terms, ("tile", "nest", "lev")), 0)
         boundary = lax.dynamic_slice_in_dim(totals, nest_at * slot_count, slot_count, 0)
         boundary = boundary.reshape(slot_count, fields, level_count, 4, BWP, FP)
         south_full = across(boundary[:, :, :, 0], south_index)

time: 801 us -> 703 us (0.88)
  waiting for transfers between devices: 73.1 us -> 5.48 us
  other arithmetic: 168 us -> 142 us
  local copies, waits for them, and re-layouts: 416 us -> 404 us
    psum x1 -> x0, waiting for transfers between devices: 70.3 us -> none  [per_device(): totals = lax.psum(terms, ('tile', 'nest', 'lev'))]
    add x2, other arithmetic: 75.6 us -> 50.2 us  [per_device(): nests_now = relaxed + inside * change]
    gather x4, local copies, waits for them, and re-layouts: 54 us -> 33 us  [across(): return jnp.take(picked, coarse_cols, axis=4)]
    gather x1 -> x3, local copies, waits for them, and re-layouts: 0.08 us -> 12.1 us  [relocate(): lax.dynamic_slice(single, (zero_index, zero_index, reach_rows + offset[0]...]
    gather x18 -> x24, local copies, waits for them, and re-layouts: 31.2 us -> 36.3 us
    unnamed x87 -> x118, local copies, waits for them, and re-layouts: 18.4 us -> 20 us
  transfers between devices with their start and end apart: 25 -> 26, of which waited for: 4 -> 7; matrix products, arithmetic and copies ran while one was open for 28% -> 28% of each run, Pallas kernels for 0% -> 0%
where the time goes in v1:
time: 703 us; the launch traced here: 691 us
  local copies, waits for them, and re-layouts  404 us (57%)
  other arithmetic  142 us (20%)
  starting transfers between devices  75.8 us (11%)
  loops' own time  47.7 us (7%)
  between operations  15.4 us (2%)
    gather x8, local copies, waits for them, and re-layouts, along(): picked = jnp.take(picked, coarse_rows, axis=4)  66.7 us
    ppermute x12, starting transfers between devices, extended(): lax.ppermute(tail, axis, [(i, (i + 1) % count) for i in range(ends)])  59.6 us
    add x2, other arithmetic, per_device(): nests_now = relaxed + inside * change  50.2 us
    another operation x2, loops' own time, extract(): return lax.map(single, corners)  47.7 us
    gather x4, local copies, waits for them, and re-layouts, along(): picked = jnp.take(zone, zone_index, axis=3)  46.2 us
    gather x24, local copies, waits for them, and re-layouts  36.3 us
    slice x11, local copies, waits for them, and re-layouts, extended(): lax.slice_in_dim(cells, cells.shape[dim] - width, cells.shape[dim], axis=...  33.2 us
    gather x4, local copies, waits for them, and re-layouts, across(): return jnp.take(picked, coarse_cols, axis=4)  33 us
  transfers between devices with their start and end apart: 26, of which 7 were waited for; matrix products, arithmetic and copies ran while one was open for 28% of the time, Pallas kernels for 0%

profile of v1, /device:TPU:0, one launch (start us, length us, event | category | flops | bytes accessed | tf_op | source)
XLA Modules:
  0.0 690.9 jit_solution(16137449762624660267)
XLA Ops:
  9.4 5.6 collective-permute-start.1
  29.2 50.2 %while.32 = (s32[]{:T(128)}, f32[6,5,2,1024]{3,2,1,0:T(2,128)S(1)}, s32[6,2]{0,1:T(2,128)S(1)}, f32[5,2,320,384]{2,3,1,0:T(8,128)}, s32[]{:T(128)}, /*index=5*/s...) while((s32[]{:T(128)}, f32[6,5,2,1024]{3,2,1,0:T(2,128)S(1)}, ...), condition=%wide.region_5.6_spmd, body=%wide.region_4.5_spmd.sunk | while | flops 40981 | bytes 450935 | solution.py:92
  81.5 5.5 collective-permute-start.5
  89.8 6.1 collective-permute-start.7
  101.6 50.0 %while.33 = (s32[]{:T(128)}, f32[6,5,2,1024]{3,2,1,0:T(2,128)S(1)}, s32[6,2]{0,1:T(2,128)S(1)}, f32[5,2,320,384]{2,3,1,0:T(8,128)}, s32[]{:T(128)}, /*index=5*/s...) while((s32[]{:T(128)}, f32[6,5,2,1024]{3,2,1,0:T(2,128)S(1)}, ...), condition=%wide.region_9.14_spmd, body=%wide.region_8.13_spmd.sunk | while | flops 40981 | bytes 450935 | solution.py:92
  154.9 5.2 collective-permute-start.8
  182.9 10.1 %collective-permute-start.10 = (f32[3,5,2,108,6]{3,2,4,1,0:T(2,128)S(1)}, f32[3,5,2,108,6]{3,2,4,1,0:T(2,128)S(1)}, u32[]{:S(2)}, u32[]{:S(2)}) collective-permute-start(f32[3,5,2,108,6]{3,2,4,1,0:T(2,128)S(1)} %get-tuple-element.419), channel_id=1, source_target_pairs={{0,1},{2,3},{4,5},{6,7},{8,9},{10,11},{12,13},{14,15},{16,17},{18,... | collective-permute-start | bytes 233288 | tf_op jit(solution)/shard_map/ppermute | solution.py:19
  193.8 7.4 %pad_maximum_fusion.17 = f32[3,5,2,108,204]{3,2,4,1,0:T(2,128)} fusion(f32[3,5,2,108,6]{3,2,4,1,0:T(2,128)S(1)} %collective-permute-done.11, f32[3,5,2,6,192]{3,2,4,1,0:T(2,128)S(1)} %copy-done.6, f32[3,5,2,96,192]{3,2,4,1,0:T(2,128)S(1)} %copy.340, f32[3,5,2,6,192]{3,2,4,1,0:T(2,128)S(1)} %copy-done.7, f32[3,5,2,108,6]{3,2,4,1,0:T(2,128)S(1)} %collective-permute-done.10), kind=kLoop, calls=%fused_computation.97 | loop fusion | flops 2643840 | bytes 5287680 | tf_op jit(solution)/shard_map/concatenate | solution.py:17
  203.1 22.5 %while.34 = (s32[]{:T(128)}, f32[3,5,2,108,204]{3,2,4,1,0:T(2,128)}, s32[3,5]{1,0:T(4,128)}, f32[3,5,2,96,192]{4,3,2,1,0:T(8,128)}, s32[]{:T(128)}) while((s32[]{:T(128)}, f32[3,5,2,108,204]{3,2,4,1,0:T(2,128)}, s32[3,5]{1,0:T(4,128)}, f32[3,5,2,96,192]{4,3,2,1,0:T(8,128)}, s32[]{:T(128)}) %tuple.212), condition=%wide.while_cond, body=%wide.while_body.sunk | while | flops 2 | bytes 4669593 | solution.py:132
  225.7 5.9 copy.357
  239.0 12.4 %gather_fusion.14 = f32[192,3,5,2,128]{4,3,2,1,0:T(2,128)S(1)} fusion(f32[3,5,2,2,128]{4,2,3,1,0:T(2,128)S(1)} %bitcast.168, s32[1024]{0:T(1024)S(1)} %pad_clamp_fusion), kind=kCustom, calls=%fused_computation.12.clone | custom fusion | bytes 5899008 | tf_op jit(solution)/shard_map/jit(_take)/gather | solution.py:143
  251.5 11.0 %gather_fusion.6 = f32[192,3,5,2,128]{4,3,2,1,0:T(2,128)} fusion(f32[3,5,2,2,128]{4,2,3,1,0:T(2,128)S(1)} %bitcast.169, s32[1024]{0:T(1024)S(1)} %pad_clamp_fusion), kind=kCustom, calls=%fused_computation.10.clone | custom fusion | bytes 5899008 | tf_op jit(solution)/shard_map/jit(_take)/gather | solution.py:143
  262.5 6.9 select_bitcast_fusion
  269.4 8.0 %copy.355 = f32[3,5,2,192,128]{3,2,4,1,0:T(2,128)} copy(f32[3,5,2,192,128]{4,2,1,0,3:T(2,128)} %get-tuple-element.471) | data formatting | bytes 5898240 | tf_op jit(solution)/shard_map/jit(_take)/select_n | solution.py:143
  277.3 11.4 %gather_fusion.7 = f32[96,3,5,2,192]{4,3,2,1,0:T(2,128)S(1)} fusion(f32[3,5,2,192,128]{3,2,4,1,0:T(2,128)} %copy.355, s32[1024]{0:T(1024)S(1)} %pad_clamp_fusion.1), kind=kCustom, calls=%fused_computation.13.clone | custom fusion | bytes 4424064 | tf_op jit(solution)/shard_map/jit(_take)/gather | solution.py:144
  288.7 5.2 copy.356
  294.0 11.8 %gather_fusion.12 = f32[192,3,5,2,128]{4,3,2,1,0:T(2,128)S(1)} fusion(f32[3,5,2,2,128]{4,2,3,1,0:T(2,128)S(1)} %bitcast.171, s32[1024]{0:T(1024)S(1)} %pad_clamp_fusion.2), kind=kCustom, calls=%fused_computation.11.clone | custom fusion | bytes 5899008 | tf_op jit(solution)/shard_map/jit(_take)/gather | solution.py:143
  305.9 10.9 %gather_fusion.4 = f32[192,3,5,2,128]{4,3,2,1,0:T(2,128)} fusion(f32[3,5,2,2,128]{4,2,3,1,0:T(2,128)S(1)} %bitcast.170, s32[1024]{0:T(1024)S(1)} %pad_clamp_fusion.2), kind=kCustom, calls=%fused_computation.2.clone | custom fusion | bytes 5899008 | tf_op jit(solution)/shard_map/jit(_take)/gather | solution.py:143
  316.7 6.9 select_bitcast_fusion.1
  323.6 8.0 %copy.352 = f32[3,5,2,192,128]{3,2,4,1,0:T(2,128)} copy(f32[3,5,2,192,128]{4,2,1,0,3:T(2,128)} %get-tuple-element.469) | data formatting | bytes 5898240 | tf_op jit(solution)/shard_map/jit(_take)/select_n | solution.py:143
  331.6 11.0 %gather_fusion.5 = f32[96,3,5,2,192]{4,3,2,1,0:T(2,128)S(1)} fusion(f32[3,5,2,192,128]{3,2,4,1,0:T(2,128)} %copy.352, s32[1024]{0:T(1024)S(1)} %pad_clamp_fusion.1), kind=kCustom, calls=%fused_computation.3.clone | custom fusion | bytes 4424064 | tf_op jit(solution)/shard_map/jit(_take)/gather | solution.py:144
  342.6 5.5 copy.353
  367.2 5.0 select_bitcast_fusion.5
  376.6 12.3 %gather_fusion.3 = f32[192,3,5,2,96]{4,3,2,1,0:T(2,128)} fusion(f32[3,5,2,96,128]{3,2,4,1,0:T(2,128)S(1)} %copy.349, s32[1024]{0:T(1024)S(1)} %pad_clamp_fusion.4), kind=kCustom, calls=%fused_computation.7.clone | custom fusion | bytes 4424448 | tf_op jit(solution)/shard_map/jit(_take)/gather | solution.py:140
  388.9 5.0 gather_fusion.1
  394.0 7.7 %multiply_add_fusion.1 = f32[3,5,2,96,192]{3,1,2,0,4:T(8,128)S(1)} fusion(f32[3,5,2,96,192]{3,1,2,0,4:T(8,128)} %copy.357, f32[96,3,5,2,192]{0,2,3,1,4:T(8,128)} %copy.356, f32[96,3,5,2,192]{0,2,3,1,4:T(8,128)} %copy.353, f32[192,3,5,2,96]{4,3,2,1,0:T(2,128)S(1)} %copy-done.9, f32[192,3,5,2,96]{4,2,3,1,0:T(8,128)} %gather_fusion.1, ...), kind=kLoop, calls=%fused_computation.96 | loop fusion | flops 6635520 | bytes 13400928 | tf_op jit(solution)/shard_map/add | solution.py:177
  401.7 5.1 fusion.60
  415.8 4.5 collective-permute-start.13
  434.7 5.6 select_maximum_fusion.4
  440.3 24.9 %fusion.15 = f32[3,5,2,96,192]{3,1,2,0,4:T(8,128)} fusion(f32[3,5,2,96,192]{3,1,2,0,4:T(8,128)S(1)} %bitcast.175, f32[3,5,4,98,194]{3,1,2,0,4:T(8,128)} %select_maximum_fusion.4, f32[3,5,2,98,1]{3,1,2,0,4:T(8,128)S(1)} %collective-permute-done.15, f32[3,5,2,1,192]{3,1,2,0,4:T(8,128)} %copy.359, f32[3,5,2,1,192]{3,1,2,0,4:T(8,128)} %copy.361, ...), kind=kLoop, calls=%fused_computation.71 | loop fusion | flops 11612160 | bytes 8990728 | tf_op jit(solution)/shard_map/add | solution.py:181
  465.2 8.9 %fusion.59 = (f32[3,5,2,6,192]{3,1,2,0,4:T(8,128)}, f32[3,5,2,6,192]{3,1,2,0,4:T(8,128)}) fusion(f32[3,5,2,96,192]{3,1,2,0,4:T(8,128)} %fusion.15), kind=kLoop, calls=%fused_computation.263 | loop fusion | bytes 552960 | tf_op jit(solution)/shard_map/slice | solution.py:16
  483.2 4.5 collective-permute-start.16
  503.8 6.1 copy.381
  510.0 10.7 %gather_fusion.15 = f32[96,3,5,2,192]{4,3,2,1,0:T(2,128)} fusion(f32[3,5,2,192,128]{3,2,4,1,0:T(2,128)} %copy.381, s32[1024]{0:T(1024)S(1)} %pad_clamp_fusion.1), kind=kCustom, calls=%fused_computation.15.clone | custom fusion | bytes 4424064 | tf_op jit(solution)/shard_map/jit(_take)/gather | solution.py:144
  520.7 6.8 copy.382
  527.4 5.8 copy.378
  533.3 11.0 %gather_fusion.13 = f32[96,3,5,2,192]{4,3,2,1,0:T(2,128)S(1)} fusion(f32[3,5,2,192,128]{3,2,4,1,0:T(2,128)} %copy.378, s32[1024]{0:T(1024)S(1)} %pad_clamp_fusion.1), kind=kCustom, calls=%fused_computation.14.clone | custom fusion | bytes 4424064 | tf_op jit(solution)/shard_map/jit(_take)/gather | solution.py:144
  544.2 5.2 copy.379
  553.0 12.5 %gather_fusion.11 = f32[192,3,5,2,96]{4,3,2,1,0:T(2,128)} fusion(f32[3,5,2,96,128]{3,2,4,1,0:T(2,128)S(1)} %copy.375, s32[1024]{0:T(1024)S(1)} %pad_clamp_fusion.4), kind=kCustom, calls=%fused_computation.9.clone | custom fusion | bytes 4424448 | tf_op jit(solution)/shard_map/jit(_take)/gather | solution.py:140
  571.7 8.0 %pad_maximum_fusion = f32[3,5,2,108,204]{3,1,2,0,4:T(8,128)} fusion(f32[3,5,2,108,6]{3,1,2,0,4:T(8,128)S(1)} %collective-permute-done.19, f32[3,5,2,6,192]{3,1,2,0,4:T(8,128)} %copy.367, f32[3,5,2,96,192]{3,1,2,0,4:T(8,128)} %fusion.15, f32[3,5,2,6,192]{3,1,2,0,4:T(8,128)} %copy.366, f32[3,5,2,108,6]{3,1,2,0,4:T(8,128)} %collective-permute-done.18), kind=kLoop, calls=%fused_computation.46 | loop fusion | flops 2643840 | bytes 5287680 | tf_op jit(solution)/shard_map/concatenate | solution.py:17
  585.7 13.8 %while.35 = (s32[]{:T(128)}, f32[3,5,2,108,204]{4,3,2,1,0:T(8,128)S(1)}, s32[3,5]{1,0:T(4,128)}, f32[3,5,2,96,192]{4,3,2,1,0:T(8,128)}, s32[]{:T(128)}) while((s32[]{:T(128)}, f32[3,5,2,108,204]{4,3,2,1,0:T(8,128)S(1)}, s32[3,5]{1,0:T(4,128)}, f32[3,5,2,96,192]{4,3,2,1,0:T(8,128)}, s32[]{:T(128)}) %tuple.221), condition=%wide.while_cond.1, body=%wide.while_body.1.sunk | while | flops 2 | bytes 1721997 | solution.py:132
  599.6 6.1 copy.383
  605.7 7.7 %multiply_add_fusion = f32[3,5,2,96,192]{3,1,2,0,4:T(8,128)S(1)} fusion(f32[3,5,2,96,192]{3,1,2,0,4:T(8,128)} %copy.383, f32[96,3,5,2,192]{0,2,3,1,4:T(8,128)} %copy.382, f32[96,3,5,2,192]{0,2,3,1,4:T(8,128)} %copy.379, f32[192,3,5,2,96]{4,3,2,1,0:T(2,128)S(1)} %copy-done.8, f32[192,3,5,2,96]{4,2,3,1,0:T(8,128)} %gather_fusion.9, ...), kind=kLoop, calls=%fused_computation.95 | loop fusion | flops 6635520 | bytes 13400928 | tf_op jit(solution)/shard_map/add | solution.py:177
  613.5 5.1 fusion.58
  627.8 5.0 collective-permute-start.21
  647.3 5.8 select_maximum_fusion
  653.1 25.2 %fusion.5 = f32[3,5,2,96,192]{3,1,2,0,4:T(8,128)} fusion(f32[3,5,2,96,192]{3,1,2,0,4:T(8,128)S(1)} %bitcast.173, f32[3,5,4,98,194]{3,1,2,0,4:T(8,128)} %select_maximum_fusion, f32[3,5,2,98,1]{3,1,2,0,4:T(8,128)S(1)} %collective-permute-done.23, f32[3,5,2,1,192]{3,1,2,0,4:T(8,128)} %copy.385, f32[3,5,2,1,192]{3,1,2,0,4:T(8,128)} %copy.387, ...), kind=kLoop, calls=%fused_computation.52 | loop fusion | flops 11612160 | bytes 8990728 | tf_op jit(solution)/shard_map/add | solution.py:181
  678.3 5.5 copy.390
  (406 shorter events, 262.8 us)
Async XLA Ops:
  7.2 18.0 %copy-start.12 = (f32[5,2,64,128]{3,2,1,0:T(8,128)S(1)}, f32[5,2,64,128]{3,2,1,0:T(8,128)}, u32[]{:S(2)}) copy-start(f32[5,2,64,128]{3,2,1,0:T(8,128)} %param.18) | copy-start | bytes 983044
  7.2 18.0 %copy-start.21 = (f32[5]{0:T(128)S(1)}, f32[5]{0:T(128)}, u32[]{:S(2)}) copy-start(f32[5]{0:T(128)} %param.21) | copy-start | bytes 64
  7.2 18.0 %copy-start.22 = (f32[5]{0:T(128)S(1)}, f32[5]{0:T(128)}, u32[]{:S(2)}) copy-start(f32[5]{0:T(128)} %param.20) | copy-start | bytes 64
  7.2 224.4 %all-gather.5.cloned.1.call-start = ((), (), s32[]{:S(2)}) async-start(), calls=%async_computation | async-start | bytes 4177920 | tf_op jit(solution)/shard_map/all_gather | solution.py:157
  8.1 8.9 %collective-permute-start = (f32[5,2,1,128]{3,2,1,0:T(1,128)S(1)}, f32[5,2,1,128]{3,2,1,0:T(1,128)S(1)}, u32[]{:S(2)}, u32[]{:S(2)}) collective-permute-start(f32[5,2,1,128]{3,2,1,0:T(1,128)S(1)} %get-tuple-element.436), channel_id=1, source_target_pairs={{4,0},{8,4},{12,8},{5,1},{9,5},{13,9},{6,2},{10,6},{14,10},{7,3},{... | collective-permute-start | bytes 15368 | tf_op jit(solution)/shard_map/ppermute | solution.py:21
  9.4 7.6 %collective-permute-start.1 = (f32[5,2,1,128]{3,2,1,0:T(1,128)S(1)}, f32[5,2,1,128]{3,2,1,0:T(1,128)S(1)}, u32[]{:S(2)}, u32[]{:S(2)}) collective-permute-start(f32[5,2,1,128]{3,2,1,0:T(1,128)S(1)} %get-tuple-element.435), channel_id=1, source_target_pairs={{0,4},{4,8},{8,12},{1,5},{5,9},{9,13},{2,6},{6,10},{10,14},{3,7},{... | collective-permute-start | bytes 15368 | tf_op jit(solution)/shard_map/ppermute | solution.py:19
  18.2 4.4 collective-permute-start.2
  19.5 4.3 collective-permute-start.3
  80.1 154.9 %all-gather.7.cloned.1.call-start = ((), (), s32[]{:S(2)}) async-start(), calls=%async_computation.1 | async-start | bytes 4177920 | tf_op jit(solution)/shard_map/all_gather | solution.py:157
  80.2 7.1 %collective-permute-start.4 = (f32[5,2,1,128]{3,2,1,0:T(1,128)S(1)}, f32[5,2,1,128]{3,2,1,0:T(1,128)S(1)}, u32[]{:S(2)}, u32[]{:S(2)}) collective-permute-start(f32[5,2,1,128]{3,2,1,0:T(1,128)S(1)} %get-tuple-element.434), channel_id=1, source_target_pairs={{4,0},{8,4},{12,8},{5,1},{9,5},{13,9},{6,2},{10,6},{14,10},{7,3},{... | collective-permute-start | bytes 15368 | tf_op jit(solution)/shard_map/ppermute | solution.py:21
  81.5 6.8 collective-permute-start.5
  88.5 7.4 %collective-permute-start.6 = (f32[5,2,66,1]{3,2,1,0:T(8,128)S(1)}, f32[5,2,66,1]{3,2,1,0:T(8,128)S(1)}, u32[]{:S(2)}, u32[]{:S(2)}) collective-permute-start(f32[5,2,66,1]{3,2,1,0:T(8,128)S(1)} %get-tuple-element.430), channel_id=1, source_target_pairs={{1,0},{2,1},{3,2},{5,4},{6,5},{7,6},{9,8},{10,9},{11,10},{13,12},{... | collective-permute-start | bytes 7928 | tf_op jit(solution)/shard_map/ppermute | solution.py:21
  89.8 7.3 %collective-permute-start.7 = (f32[5,2,66,1]{3,2,1,0:T(8,128)S(1)}, f32[5,2,66,1]{3,2,1,0:T(8,128)S(1)}, u32[]{:S(2)}, u32[]{:S(2)}) collective-permute-start(f32[5,2,66,1]{3,2,1,0:T(8,128)S(1)} %get-tuple-element.429), channel_id=1, source_target_pairs={{0,1},{1,2},{2,3},{4,5},{5,6},{6,7},{8,9},{9,10},{10,11},{12,13},{... | collective-permute-start | bytes 7928 | tf_op jit(solution)/shard_map/ppermute | solution.py:19
  101.6 58.6 %copy-start.44 = (s32[6]{0:T(128)S(1)}, s32[6]{0:T(128)}, u32[]{:S(2)}) copy-start(s32[6]{0:T(128)} %param.23) | copy-start | bytes 76
  153.5 18.9 %collective-permute-start.9 = (f32[3,5,2,6,192]{4,2,3,1,0:T(2,128)S(1)}, f32[3,5,2,6,192]{4,2,3,1,0:T(2,128)S(1)}, u32[]{:S(2)}, u32[]{:S(2)}) collective-permute-start(f32[3,5,2,6,192]{4,2,3,1,0:T(2,128)S(1)} %copy.393), channel_id=1, source_target_pairs={{4,0},{8,4},{12,8},{5,1},{9,5},{13,9},{6,2},{10,6},{14,10},{7,3},{... | collective-permute-start | bytes 414728 | tf_op jit(solution)/shard_map/ppermute | solution.py:21
  154.9 20.8 %collective-permute-start.8 = (f32[3,5,2,6,192]{4,2,3,1,0:T(2,128)S(1)}, f32[3,5,2,6,192]{4,2,3,1,0:T(2,128)}, u32[]{:S(2)}, u32[]{:S(2)}) collective-permute-start(f32[3,5,2,6,192]{4,2,3,1,0:T(2,128)S(1)} %copy.392), channel_id=1, source_target_pairs={{0,4},{4,8},{8,12},{1,5},{5,9},{9,13},{2,6},{6,10},{10,14},{3,7},{... | collective-permute-start | bytes 414728 | tf_op jit(solution)/shard_map/ppermute | solution.py:19
  163.4 9.0 %copy-start.37 = (s32[96]{0:T(128)}, s32[96]{0:T(128)S(1)}, u32[]{:S(2)}) copy-start(s32[96]{0:T(128)S(1)} %get-tuple-element.493) | copy-start | bytes 1156
  179.8 13.9 %copy-start.6 = (f32[3,5,2,6,192]{3,2,4,1,0:T(2,128)S(1)}, f32[3,5,2,6,192]{3,2,4,1,0:T(2,128)}, u32[]{:S(2)}) copy-start(f32[3,5,2,6,192]{3,2,4,1,0:T(2,128)} %copy.341) | copy-start | bytes 414724
  179.8 13.9 %copy-start.7 = (f32[3,5,2,6,192]{3,2,4,1,0:T(2,128)S(1)}, f32[3,5,2,6,192]{3,2,4,1,0:T(2,128)}, u32[]{:S(2)}) copy-start(f32[3,5,2,6,192]{3,2,4,1,0:T(2,128)} %copy.339) | copy-start | bytes 414724
  181.5 12.1 %collective-permute-start.11 = (f32[3,5,2,108,6]{3,2,4,1,0:T(2,128)S(1)}, f32[3,5,2,108,6]{3,2,4,1,0:T(2,128)S(1)}, u32[]{:S(2)}, u32[]{:S(2)}) collective-permute-start(f32[3,5,2,108,6]{3,2,4,1,0:T(2,128)S(1)} %get-tuple-element.420), channel_id=1, source_target_pairs={{1,0},{3,2},{5,4},{7,6},{9,8},{11,10},{13,12},{15,14},{17,16},{19,... | collective-permute-start | bytes 233288 | tf_op jit(solution)/shard_map/ppermute | solution.py:21
  182.9 10.9 %collective-permute-start.10 = (f32[3,5,2,108,6]{3,2,4,1,0:T(2,128)S(1)}, f32[3,5,2,108,6]{3,2,4,1,0:T(2,128)S(1)}, u32[]{:S(2)}, u32[]{:S(2)}) collective-permute-start(f32[3,5,2,108,6]{3,2,4,1,0:T(2,128)S(1)} %get-tuple-element.419), channel_id=1, source_target_pairs={{0,1},{2,3},{4,5},{6,7},{8,9},{10,11},{12,13},{14,15},{16,17},{18,... | collective-permute-start | bytes 233288 | tf_op jit(solution)/shard_map/ppermute | solution.py:19
  239.0 23.5 %copy-start.43 = (pred[192]{0:T(512)(128)(4,1)S(1)}, pred[192]{0:T(512)(128)(4,1)}, u32[]{:S(2)}) copy-start(pred[192]{0:T(512)(128)(4,1)} %get-tuple-element.488) | copy-start | bytes 580
  294.0 22.7 %copy-start.42 = (pred[192]{0:T(512)(128)(4,1)S(1)}, pred[192]{0:T(512)(128)(4,1)}, u32[]{:S(2)}) copy-start(pred[192]{0:T(512)(128)(4,1)} %get-tuple-element.489) | copy-start | bytes 580
  356.8 10.4 %copy-start.40 = (pred[96]{0:T(512)(128)(4,1)S(1)}, pred[96]{0:T(512)(128)(4,1)}, u32[]{:S(2)}) copy-start(pred[96]{0:T(512)(128)(4,1)} %get-tuple-element.476) | copy-start | bytes 292
  376.5 17.4 %copy-start.16 = (f32[96,192]{0,1:T(8,128)S(1)}, f32[96,192]{0,1:T(8,128)}, u32[]{:S(2)}) copy-start(f32[96,192]{0,1:T(8,128)} %fusion.46) | copy-start | bytes 221188
  376.5 17.4 %copy-start.19 = (pred[3,96,192]{1,0,2:T(4,128)(4,1)S(1)}, pred[3,96,192]{1,0,2:T(4,128)(4,1)}, u32[]{:S(2)}) copy-start(pred[3,96,192]{1,0,2:T(4,128)(4,1)} %broadcast_and_fusion) | copy-start | bytes 165892
  376.5 17.4 %copy-start.25 = (pred[96]{0:T(512)(128)(4,1)S(1)}, pred[96]{0:T(512)(128)(4,1)}, u32[]{:S(2)}) copy-start(pred[96]{0:T(512)(128)(4,1)} %get-tuple-element.474) | copy-start | bytes 292
  376.5 17.4 %copy-start.27 = (pred[96]{0:T(512)(128)(4,1)S(1)}, pred[96]{0:T(512)(128)(4,1)}, u32[]{:S(2)}) copy-start(pred[96]{0:T(512)(128)(4,1)} %get-tuple-element.477) | copy-start | bytes 292
  376.5 17.4 %copy-start.29 = (pred[192]{0:T(512)(128)(4,1)S(1)}, pred[192]{0:T(512)(128)(4,1)}, u32[]{:S(2)}) copy-start(pred[192]{0:T(512)(128)(4,1)} %get-tuple-element.490) | copy-start | bytes 580
  376.5 17.4 %copy-start.31 = (pred[192]{0:T(512)(128)(4,1)S(1)}, pred[192]{0:T(512)(128)(4,1)}, u32[]{:S(2)}) copy-start(pred[192]{0:T(512)(128)(4,1)} %get-tuple-element.491) | copy-start | bytes 580
  376.5 17.4 %copy-start.33 = (pred[192]{0:T(512)(128)(4,1)S(1)}, pred[192]{0:T(512)(128)(4,1)}, u32[]{:S(2)}) copy-start(pred[192]{0:T(512)(128)(4,1)} %broadcast_compare_fusion.1) | copy-start | bytes 580
  376.6 17.4 %copy-start.35 = (pred[96]{0:T(512)(128)(4,1)S(1)}, pred[96]{0:T(512)(128)(4,1)}, u32[]{:S(2)}) copy-start(pred[96]{0:T(512)(128)(4,1)} %broadcast_compare_fusion.3) | copy-start | bytes 292
  410.7 9.7 %collective-permute-start.12 = (f32[3,5,2,1,192]{4,2,3,1,0:T(2,128)S(1)}, f32[3,5,2,1,192]{4,2,3,1,0:T(2,128)S(1)}, u32[]{:S(2)}, u32[]{:S(2)}) collective-permute-start(f32[3,5,2,1,192]{4,2,3,1,0:T(2,128)S(1)} %copy.358), channel_id=1, source_target_pairs={{4,0},{8,4},{12,8},{5,1},{9,5},{13,9},{6,2},{10,6},{14,10},{7,3},{... | collective-permute-start | bytes 69128 | tf_op jit(solution)/shard_map/ppermute | solution.py:21
  415.8 8.4 %collective-permute-start.13 = (f32[3,5,2,1,192]{4,2,3,1,0:T(2,128)S(1)}, f32[3,5,2,1,192]{4,2,3,1,0:T(2,128)S(1)}, u32[]{:S(2)}, u32[]{:S(2)}) collective-permute-start(f32[3,5,2,1,192]{4,2,3,1,0:T(2,128)S(1)} %copy.360), channel_id=1, source_target_pairs={{0,4},{4,8},{8,12},{1,5},{5,9},{9,13},{2,6},{6,10},{10,14},{3,7},{... | collective-permute-start | bytes 69128 | tf_op jit(solution)/shard_map/ppermute | solution.py:19
  424.2 10.5 %slice-start.2 = ((s8[4718592]{0:T(1024)(128)(4,1)}), s8[524288]{0:T(1024)(128)(4,1)S(1)}, s32[]{:S(2)}) async-start(s8[4718592]{0:T(1024)(128)(4,1)} %bitcast.174), calls=%async_computation.4 | async-start | bytes 1048576
  429.1 4.9 collective-permute-start.14
  430.7 4.0 collective-permute-start.15
  474.1 13.6 %copy-start.24 = (pred[3,192]{1,0:T(4,128)(4,1)S(1)}, pred[3,192]{1,0:T(4,128)(4,1)}, u32[]{:S(2)}) copy-start(pred[3,192]{1,0:T(4,128)(4,1)} %get-tuple-element.460) | copy-start | bytes 1732
  478.0 9.9 %collective-permute-start.17 = (f32[3,5,2,6,192]{4,2,3,1,0:T(2,128)S(1)}, f32[3,5,2,6,192]{4,2,3,1,0:T(2,128)S(1)}, u32[]{:S(2)}, u32[]{:S(2)}) collective-permute-start(f32[3,5,2,6,192]{4,2,3,1,0:T(2,128)S(1)} %copy.365), channel_id=1, source_target_pairs={{4,0},{8,4},{12,8},{5,1},{9,5},{13,9},{6,2},{10,6},{14,10},{7,3},{... | collective-permute-start | bytes 414728 | tf_op jit(solution)/shard_map/ppermute | solution.py:21
  483.2 8.7 %collective-permute-start.16 = (f32[3,5,2,6,192]{4,2,3,1,0:T(2,128)S(1)}, f32[3,5,2,6,192]{4,2,3,1,0:T(2,128)S(1)}, u32[]{:S(2)}, u32[]{:S(2)}) collective-permute-start(f32[3,5,2,6,192]{4,2,3,1,0:T(2,128)S(1)} %copy.364), channel_id=1, source_target_pairs={{0,4},{4,8},{8,12},{1,5},{5,9},{9,13},{2,6},{6,10},{10,14},{3,7},{... | collective-permute-start | bytes 414728 | tf_op jit(solution)/shard_map/ppermute | solution.py:19
  497.9 73.8 %collective-permute-start.19 = (f32[3,5,2,108,6]{3,1,2,0,4:T(8,128)}, f32[3,5,2,108,6]{3,1,2,0,4:T(8,128)S(1)}, u32[]{:S(2)}, u32[]{:S(2)}) collective-permute-start(f32[3,5,2,108,6]{3,1,2,0,4:T(8,128)} %get-tuple-element.416), channel_id=1, source_target_pairs={{1,0},{3,2},{5,4},{7,6},{9,8},{11,10},{13,12},{15,14},{17,16},{19,... | collective-permute-start | bytes 233288 | tf_op jit(solution)/shard_map/ppermute | solution.py:21
  499.2 72.5 %collective-permute-start.18 = (f32[3,5,2,108,6]{3,1,2,0,4:T(8,128)S(1)}, f32[3,5,2,108,6]{3,1,2,0,4:T(8,128)}, u32[]{:S(2)}, u32[]{:S(2)}) collective-permute-start(f32[3,5,2,108,6]{3,1,2,0,4:T(8,128)S(1)} %get-tuple-element.415), channel_id=1, source_target_pairs={{0,1},{2,3},{4,5},{6,7},{8,9},{10,11},{12,13},{14,15},{16,17},{18,... | collective-permute-start | bytes 233288 | tf_op jit(solution)/shard_map/ppermute | solution.py:19
  622.5 10.3 %collective-permute-start.20 = (f32[3,5,2,1,192]{4,2,3,1,0:T(2,128)S(1)}, f32[3,5,2,1,192]{4,2,3,1,0:T(2,128)S(1)}, u32[]{:S(2)}, u32[]{:S(2)}) collective-permute-start(f32[3,5,2,1,192]{4,2,3,1,0:T(2,128)S(1)} %copy.384), channel_id=1, source_target_pairs={{4,0},{8,4},{12,8},{5,1},{9,5},{13,9},{6,2},{10,6},{14,10},{7,3},{... | collective-permute-start | bytes 69128 | tf_op jit(solution)/shard_map/ppermute | solution.py:21
  627.8 8.9 %collective-permute-start.21 = (f32[3,5,2,1,192]{4,2,3,1,0:T(2,128)S(1)}, f32[3,5,2,1,192]{4,2,3,1,0:T(2,128)S(1)}, u32[]{:S(2)}, u32[]{:S(2)}) collective-permute-start(f32[3,5,2,1,192]{4,2,3,1,0:T(2,128)S(1)} %copy.386), channel_id=1, source_target_pairs={{0,4},{4,8},{8,12},{1,5},{5,9},{9,13},{2,6},{6,10},{10,14},{3,7},{... | collective-permute-start | bytes 69128 | tf_op jit(solution)/shard_map/ppermute | solution.py:19
  636.7 10.6 %slice-start = ((s8[4718592]{0:T(1024)(128)(4,1)}), s8[524288]{0:T(1024)(128)(4,1)S(1)}, s32[]{:S(2)}) async-start(s8[4718592]{0:T(1024)(128)(4,1)} %bitcast.172), calls=%async_computation.2 | async-start | bytes 1048576
  641.7 4.7 collective-permute-start.22
  643.3 9.8 %copy-start.18 = (f32[96,192]{0,1:T(8,128)S(1)}, f32[96,192]{0,1:T(8,128)}, u32[]{:S(2)}) copy-start(f32[96,192]{0,1:T(8,128)} %copy-done.17) | copy-start | bytes 221188
  643.3 4.0 collective-permute-start.23
  (28 other events, 161.6 us)
Sparse Core Ops, SparseCore 0:
  80.3 57.8 all-gather.4
  152.4 59.8 all-gather.6
